TPU v7x, 1024 devices: a whole 4x4x32 slice. The times are simulated.
1024 devices in a mesh: dp: 64 (over x, z_lo), mp: 16 (over z_hi, y, core).
Axes of the slice: x: 4, y: 4, z: 32 (z_hi: 2, z_lo: 16; z = z_hi * 16 + z_lo), core: 2. Of those that a mesh axis runs over, the one named last changes fastest.
Arguments:
- cotangent: bfloat16 [49152, 4096], P('dp'), may hold values from -6 to 6
- activations: bfloat16 [49152, 16384], P('dp', 'mp'), may hold values from -32 to 32
- live_mask: int32 [49152], P('dp'), may hold values 0 or 1
- projector: bfloat16 [4096, 256], replicated, may hold values from -0.09375 to 0.09375
- first_moment: float32 [16384, 256], P(('mp', 'dp')), may hold values from -4 to 4
- second_moment: float32 [16384, 256], P(('mp', 'dp')), may hold values from 0.05 to 2
Outputs:
- new_first: float32 [16384, 256], P(('mp', 'dp'))
- new_second: float32 [16384, 256], P(('mp', 'dp'))
- update: bfloat16 [4096, 16384], P('dp', 'mp')
All inputs are finite; a program needn't handle non-finite values. No bound on the sum of `live_mask` on one device may be relied on, other than what follows from the above.
Results may differ from a plain program's by a relative error of at most 0.0053.
Values may be sent and summed in bfloat16 or wider, within the bound.
No kernel may reach another device: no remote copies, remote signals or barrier semaphores. Data moves between devices by JAX's collectives and lax.ppermute only.
A program may use at most 32 MiB of HBM per device.

v0:
```python
import math

import jax
import jax.numpy as jnp
from jax import lax
from jax.sharding import PartitionSpec as P

beta_one = 0.9
beta_two = 0.95
corr_one = 0.99997343860111
corr_two = 0.99407947077967
adam_eps = 1e-08


def per_device(cotangent, activations, live_mask, projector, first_moment, second_moment):
    width = projector.shape[0]
    projected = jnp.dot(cotangent, projector, preferred_element_type=jnp.float32)
    weighted = (projected * live_mask.astype(jnp.float32)[:, None]).astype(jnp.bfloat16)
    factor = 1.0 / math.sqrt(activations.shape[0] * lax.axis_size("dp"))
    term = lax.dot_general(
        activations, weighted, (((0,), (0,)), ((), ())), preferred_element_type=jnp.float32
    )
    gradient = lax.psum_scatter(term * jnp.float32(factor), "dp", scatter_dimension=0, tiled=True)
    new_first = beta_one * first_moment + (1.0 - beta_one) * gradient
    new_second = beta_two * second_moment + (1.0 - beta_two) * gradient * gradient
    direction = (new_first / corr_one / (jnp.sqrt(new_second / corr_two) + adam_eps)).astype(
        jnp.bfloat16
    )
    band = width // lax.axis_size("dp")
    proj_rows = lax.dynamic_slice_in_dim(projector, lax.axis_index("dp") * band, band, 0)
    block = lax.dot_general(
        proj_rows,
        lax.all_gather(direction, "dp", axis=0, tiled=True),
        (((1,), (1,)), ((), ())),
        preferred_element_type=jnp.float32,
    )
    update = block.astype(jnp.bfloat16)
    return (new_first, new_second, update)


def solution(mesh):
    in_specs = (
        P("dp", None),
        P("dp", "mp"),
        P("dp"),
        P(),
        P(("mp", "dp"), None),
        P(("mp", "dp"), None),
    )
    out_specs = (P(("mp", "dp"), None), P(("mp", "dp"), None), P("dp", "mp"))
    return jax.shard_map(
        per_device, mesh=mesh, in_specs=in_specs, out_specs=out_specs, check_vma=False
    )
```

profile of v0, /device:TPU:24, one launch (start us, length us, event | category | flops | bytes accessed | tf_op | source)
XLA Modules:
  0.0 1197.3 jit_solution(6889393816952968667)
XLA Ops:
  7.2 0.0 copy-start
  7.2 0.0 reduce-scatter.4.cloned.1.call-start
  7.2 0.8 convert_element_type.12
  8.1 0.7 copy-done
  8.8 6.3 fusion
  15.1 0.0 copy-start.1
  15.1 0.0 copy-start.2
  15.1 1.3 copy.25
  16.4 0.0 reduce-scatter.4.cloned.1.call-update
  16.4 791.1 %reduce-scatter.4.cloned.1.call-done = f32[16,256]{1,0:T(8,128)} async-done(((f32[1024,256]{1,0:T(8,128)}), f32[16,256]{1,0:T(8,128)}) %reduce-scatter.4.cloned.1.call-update) | async-done | bytes 16400 | tf_op jit(solution)/shard_map/reduce_scatter | solution.py:23
  807.5 0.0 copy-done.1
  807.5 0.0 copy-done.2
  807.5 1.3 divide_convert_fusion
  808.8 380.7 %all_gather.3 = bf16[1024,256]{1,0:T(8,128)(2,1)S(1)} all-gather(bf16[16,256]{1,0:T(8,128)(2,1)S(1)} %get-tuple-element.9), channel_id=1, replica_groups=mesh['dp'=64,'mp'=16] {'dp'}, dimensions={0}, use_global_device_ids=true | all-gather | bytes 532480 | tf_op jit(solution)/shard_map/all_gather | solution.py:33
  1189.5 0.9 convolution_convert_fusion
Async XLA Ops:
  7.2 1.6 copy-start
  7.2 800.3 %reduce-scatter.4.cloned.1.call-start = ((), (), s32[]{:S(2)}) async-start(), calls=%async_computation.1 | async-start | bytes 1064960 | tf_op jit(solution)/shard_map/reduce_scatter | solution.py:23
  15.1 792.4 %copy-start.1 = (f32[16,256]{1,0:T(8,128)S(1)}, f32[16,256]{1,0:T(8,128)}, u32[]{:S(2)}) copy-start(f32[16,256]{1,0:T(8,128)} %param.11) | copy-start | bytes 49156
  15.1 792.4 %copy-start.2 = (f32[16,256]{1,0:T(8,128)S(1)}, f32[16,256]{1,0:T(8,128)}, u32[]{:S(2)}) copy-start(f32[16,256]{1,0:T(8,128)} %param.10) | copy-start | bytes 49156
Sparse Core Ops, SparseCore 0:
  16.5 790.9 reduce-scatter.3
where the time goes:
time: 1200 us
  waiting for transfers between devices  791 us (66%)
  blocking collectives  381 us (32%)
  between operations  14.1 us (1%)
    reduce_scatter x1, waiting for transfers between devices, per_device(): lax.psum_scatter(term * jnp.float32(factor), 'dp', scatter_dimension=0, t...  791 us
    all_gather x1, blocking collectives, per_device(): lax.all_gather(direction, 'dp', axis=0, tiled=True)  381 us
  transfers between devices with their start and end apart: 1, of which 1 were waited for; matrix products, arithmetic and copies ran while one was open for 0% of the time, Pallas kernels for 0%

commit v1 on v0

v1 whole, which is shorter than its diff:
```python
import math

import jax
import jax.numpy as jnp
from jax import lax
from jax.experimental import pallas as pl
from jax.experimental.pallas import tpu as pltpu
from jax.sharding import PartitionSpec as P

beta_one = 0.9
beta_two = 0.95
corr_one = 0.99997343860111
corr_two = 0.99407947077967
adam_eps = 1e-08

NEAR = [[16 * x + 4 * a + b for x in range(4) for b in range(4)] for a in range(4)]
SWAP_EIGHT = [(d, d ^ 8) for d in range(64)]
SWAP_FOUR = [(d, d ^ 4) for d in range(64)]


def adam(first, second, gradient):
    new_first = beta_one * first + (1.0 - beta_one) * gradient
    new_second = beta_two * second + (1.0 - beta_two) * gradient * gradient
    direction = new_first / corr_one / (jnp.sqrt(new_second / corr_two) + adam_eps)
    return new_first, new_second, direction.astype(jnp.bfloat16)


def order_kernel(blocks_ref, update_ref):
    _, _, length = blocks_ref.shape
    rows = length // 4
    source = lax.broadcasted_iota(jnp.int32, (length, 4 * length), 0)
    target = lax.broadcasted_iota(jnp.int32, (length, 4 * length), 1)
    start = (source // rows) * length + source % rows
    for x in range(4):
        total = None
        for b in range(4):
            place = (target == start + b * rows).astype(jnp.bfloat16)
            moved = jnp.dot(blocks_ref[4 * x + b], place, preferred_element_type=jnp.float32)
            total = moved if total is None else total + moved
        update_ref[:, x * 4 * length : (x + 1) * 4 * length] = total.astype(jnp.bfloat16)


def per_device(cotangent, activations, live_mask, projector, first_moment, second_moment):
    width, rank = projector.shape
    own = lax.axis_index("dp")
    projected = jnp.dot(cotangent, projector, preferred_element_type=jnp.float32)
    weighted = (projected * live_mask.astype(jnp.float32)[:, None]).astype(jnp.bfloat16)
    factor = 1.0 / math.sqrt(activations.shape[0] * lax.axis_size("dp"))
    term = lax.dot_general(
        activations, weighted, (((0,), (0,)), ((), ())), preferred_element_type=jnp.float32
    )
    rows = term.shape[0] // 64
    term = (term * jnp.float32(factor)).astype(jnp.bfloat16)
    parts = term.reshape(4, 4, 4, rows, rank).transpose(0, 2, 1, 3, 4).reshape(16, 4 * rows, rank)
    parts = lax.all_to_all(parts, "dp", 0, 0, axis_index_groups=NEAR, tiled=True)
    partial = jnp.sum(parts.astype(jnp.float32), axis=0)

    def swap(pairs, sums, first, second, low):
        note = jnp.concatenate([sums, first, second], axis=0).astype(jnp.bfloat16)
        other = lax.ppermute(note, "dp", pairs).astype(jnp.float32)
        ends = (sums.shape[0], sums.shape[0] + first.shape[0])
        firsts, seconds = other[ends[0] : ends[1]], other[ends[1] :]

        def pair(mine, yours):
            mine, yours = mine.reshape(-1, rows, rank), yours.reshape(-1, rows, rank)
            both = jnp.stack([jnp.where(low, mine, yours), jnp.where(low, yours, mine)], axis=1)
            return both.reshape(-1, rank)

        return sums + other[: ends[0]], pair(first, firsts), pair(second, seconds)

    low_eight, low_four = (own // 8) % 2 == 0, (own // 4) % 2 == 0
    gradient, firsts, seconds = swap(SWAP_EIGHT, partial, first_moment, second_moment, low_eight)
    gradient, firsts, seconds = swap(SWAP_FOUR, gradient, firsts, seconds, low_four)
    all_first, all_second, direction = adam(firsts, seconds, gradient)
    own_far = (own // 4) % 4
    new_first = lax.dynamic_slice_in_dim(all_first, own_far * rows, rows, 0)
    new_second = lax.dynamic_slice_in_dim(all_second, own_far * rows, rows, 0)
    band = width // 64
    bands = lax.dynamic_index_in_dim(projector.reshape(4, 4, 4, band, rank), own_far, 1, False)
    blocks = lax.dot_general(
        bands.reshape(16 * band, rank), direction, (((1,), (1,)), ((), ())), preferred_element_type=jnp.float32
    ).astype(jnp.bfloat16).reshape(16, band, 4 * rows)
    blocks = lax.all_to_all(blocks, "dp", 0, 0, axis_index_groups=NEAR, tiled=True)
    update = pl.pallas_call(
        order_kernel,
        out_shape=jax.ShapeDtypeStruct((band, 64 * rows), jnp.bfloat16),
        in_specs=[pl.BlockSpec(memory_space=pltpu.VMEM)],
        out_specs=pl.BlockSpec(memory_space=pltpu.VMEM),
    )(blocks)
    return (new_first, new_second, update)


def solution(mesh):
    in_specs = (
        P("dp", None),
        P("dp", "mp"),
        P("dp"),
        P(),
        P(("mp", "dp"), None),
        P(("mp", "dp"), None),
    )
    out_specs = (P(("mp", "dp"), None), P(("mp", "dp"), None), P("dp", "mp"))
    return jax.shard_map(
        per_device, mesh=mesh, in_specs=in_specs, out_specs=out_specs, check_vma=False
    )
```

time: 1200 us -> 85.2 us (0.07)
  waiting for transfers between devices: 791 us -> 30.5 us
  blocking collectives: 381 us -> 0 us
  starting transfers between devices: 0.04 us -> 38.7 us
  between operations: 14.1 us -> 0.94 us
    reduce_scatter x1 -> x0, waiting for transfers between devices: 791 us -> none  [per_device(): lax.psum_scatter(term * jnp.float32(factor), 'dp', scatter_dimension=0, t...]
    all_gather x1 -> x0, blocking collectives: 381 us -> none  [per_device(): lax.all_gather(direction, 'dp', axis=0, tiled=True)]
    ppermute x0 -> x2, starting transfers between devices: none -> 24.9 us  [swap(): other = lax.ppermute(note, 'dp', pairs).astype(jnp.float32)]
    all_to_all x0 -> x2, waiting for transfers between devices: none -> 23.6 us  [the longest x1 16.5 us: per_device(): lax.all_to_all(parts, 'dp', 0, 0, axis_index_groups=NEAR, tiled=True)]
    all_to_all x0 -> x2, starting transfers between devices: none -> 13.7 us  [the longest x1 8.46 us: per_device(): lax.all_to_all(parts, 'dp', 0, 0, axis_index_groups=NEAR, tiled=True)]
  transfers between devices with their start and end apart: 1 -> 4, of which waited for: 1 -> 4; matrix products, arithmetic and copies ran while one was open for 0% -> 2% of each run, Pallas kernels for 0% -> 0%
where the time goes in v1:
time: 85.2 us; the launch traced here: 84.7 us
  starting transfers between devices  38.7 us (45%)
  waiting for transfers between devices  30.5 us (36%)
  matrix products  6.55 us (8%)
  local copies, waits for them, and re-layouts  5.12 us (6%)
  Pallas kernels  1.89 us (2%)
  other arithmetic  1.05 us (1%)
  between operations  0.94 us (1%)
    ppermute x2, starting transfers between devices, swap(): other = lax.ppermute(note, 'dp', pairs).astype(jnp.float32)  24.9 us
    all_to_all x1, waiting for transfers between devices, per_device(): lax.all_to_all(parts, 'dp', 0, 0, axis_index_groups=NEAR, tiled=True)  16.5 us
    all_to_all x1, starting transfers between devices, per_device(): lax.all_to_all(parts, 'dp', 0, 0, axis_index_groups=NEAR, tiled=True)  8.46 us
    all_to_all x1, waiting for transfers between devices, per_device(): lax.all_to_all(blocks, 'dp', 0, 0, axis_index_groups=NEAR, tiled=True)  7.17 us
    ppermute x2, waiting for transfers between devices, swap(): other = lax.ppermute(note, 'dp', pairs).astype(jnp.float32)  6.9 us
    dot_general x1, matrix products, per_device(): lax.dot_general(activations, weighted, (((0,), (0,)), ((), ())), preferre...  6.28 us
    all_to_all x1, starting transfers between devices, per_device(): lax.all_to_all(blocks, 'dp', 0, 0, axis_index_groups=NEAR, tiled=True)  5.28 us
    unnamed x8, local copies, waits for them, and re-layouts  2.61 us
  transfers between devices with their start and end apart: 4, of which 4 were waited for; matrix products, arithmetic and copies ran while one was open for 2% of the time, Pallas kernels for 0%

profile of v1, /device:TPU:24, one launch (start us, length us, event | category | flops | bytes accessed | tf_op | source)
XLA Modules:
  0.0 84.7 jit_solution(4018117152972431230)
XLA Ops:
  0.6 0.0 copy-start
  0.6 0.8 convert_element_type.29
  1.5 0.8 copy-done
  2.2 6.3 %fusion.2 = bf16[1024,256]{0,1:T(8,128)(2,1)S(1)} fusion(bf16[768,1024]{1,0:T(8,128)(2,1)} %param.7, bf16[768,4096]{1,0:T(8,128)(2,1)} %param.6, bf16[4096,256]{1,0:T(8,128)(2,1)S(1)} %copy-done, f32[768]{0:T(1024)S(1)} %convert_element_type.29), kind=kOutput, calls=%fused_computation.4 | convolution fusion | flops 2014183424 | bytes 10488832 | tf_op jit(solution)/shard_map/dot_general | solution.py:49
  8.5 0.0 copy-start.2
  8.5 0.0 copy-start.1
  8.5 0.2 copy.10
  8.8 0.9 %copy.11 = bf16[4,4,4,16,256]{4,3,2,1,0:T(8,128)(2,1)} copy(bf16[4,4,4,16,256]{4,3,1,2,0:T(8,128)(2,1)S(1)} %bitcast.37) | data formatting | bytes 1048576 | tf_op jit(solution)/shard_map/transpose | solution.py:54
  9.6 8.5 %all-to-all-start = ((bf16[16,64,256]{2,1,0:T(8,128)(2,1)}), bf16[16,64,256]{2,1,0:T(8,128)(2,1)S(1)}, u32[]{:S(2)}, u32[]{:S(2)}) async-start(bf16[16,64,256]{2,1,0:T(8,128)(2,1)} %bitcast.3), calls=%async_computation | async-start | bytes 1048576 | tf_op jit(solution)/shard_map/all_to_all | solution.py:55
  18.1 0.0 copy-done.2
  18.1 0.0 copy-done.1
  18.1 16.5 %all-to-all-done = bf16[16,64,256]{2,1,0:T(8,128)(2,1)S(1)} async-done(((bf16[16,64,256]{2,1,0:T(8,128)(2,1)}), bf16[16,64,256]{2,1,0:T(8,128)(2,1)S(1)}, u32[]{:S(2)}, u32[]{:S(2)}) %all-to-all-start) | async-done | bytes 524320 | tf_op jit(solution)/shard_map/all_to_all | solution.py:55
  34.6 0.1 convert_reduce_fusion
  34.7 15.7 %collective-permute-start = (bf16[96,256]{1,0:T(8,128)(2,1)S(1)}, bf16[96,256]{1,0:T(8,128)(2,1)S(1)}, u32[]{:S(2)}, u32[]{:S(2)}) collective-permute-start(bf16[96,256]{1,0:T(8,128)(2,1)S(1)} %pad_maximum_fusion.1), channel_id=1, source_target_pairs={{0,128},{16,144},{32,160},{48,176},{64,192},{80,208},{96,224},{112... | collective-permute-start | bytes 147464 | tf_op jit(solution)/shard_map/ppermute | solution.py:60
  50.5 2.4 %collective-permute-done = bf16[96,256]{1,0:T(8,128)(2,1)S(1)} collective-permute-done((bf16[96,256]{1,0:T(8,128)(2,1)S(1)}, bf16[96,256]{1,0:T(8,128)(2,1)S(1)}, u32[]{:S(2)}, u32[]{:S(2)}) %collective-permute-start) | collective-permute-done | bytes 49184 | tf_op jit(solution)/shard_map/ppermute | solution.py:60
  53.0 9.2 %collective-permute-start.1 = (bf16[128,256]{1,0:T(8,128)(2,1)S(1)}, bf16[128,256]{1,0:T(8,128)(2,1)S(1)}, u32[]{:S(2)}, u32[]{:S(2)}) collective-permute-start(bf16[128,256]{1,0:T(8,128)(2,1)S(1)} %pad_maximum_fusion), channel_id=1, source_target_pairs={{0,64},{16,80},{32,96},{48,112},{64,0},{80,16},{96,32},{112,48},{1... | collective-permute-start | bytes 196616 | tf_op jit(solution)/shard_map/ppermute | solution.py:60
  62.2 4.5 %collective-permute-done.1 = bf16[128,256]{1,0:T(8,128)(2,1)S(1)} collective-permute-done((bf16[128,256]{1,0:T(8,128)(2,1)S(1)}, bf16[128,256]{1,0:T(8,128)(2,1)S(1)}, u32[]{:S(2)}, u32[]{:S(2)}) %collective-permute-start.1) | collective-permute-done | bytes 65568 | tf_op jit(solution)/shard_map/ppermute | solution.py:60
  66.9 0.3 convolution_convert_fusion
  67.2 0.2 copy.14
  67.3 0.9 %reshape.132 = bf16[16,2,2048]{2,1,0:T(2,128)(2,1)} reshape(bf16[16,64,64]{2,1,0:T(8,128)(2,1)S(1)} %bitcast.38) | data formatting | bytes 262144
  68.2 5.3 %all-to-all-start.1 = ((bf16[16,2,2048]{2,1,0:T(2,128)(2,1)}), bf16[16,2,2048]{2,1,0:T(2,128)(2,1)S(1)}, u32[]{:S(2)}, u32[]{:S(2)}) async-start(bf16[16,2,2048]{2,1,0:T(2,128)(2,1)} %reshape.132), calls=%async_computation.1 | async-start | bytes 262144 | tf_op jit(solution)/shard_map/all_to_all | solution.py:83
  73.5 0.6 constant_dynamic-slice_fusion.2
  74.1 0.6 constant_dynamic-slice_fusion.1
  74.8 7.2 %all-to-all-done.1 = bf16[16,2,2048]{2,1,0:T(2,128)(2,1)S(1)} async-done(((bf16[16,2,2048]{2,1,0:T(2,128)(2,1)}), bf16[16,2,2048]{2,1,0:T(2,128)(2,1)S(1)}, u32[]{:S(2)}, u32[]{:S(2)}) %all-to-all-start.1) | async-done | bytes 131104 | tf_op jit(solution)/shard_map/all_to_all | solution.py:83
  81.9 0.9 %reshape.133.blocks_ref = bf16[16,64,64]{2,1,0:T(8,128)(2,1)} reshape(bf16[16,2,2048]{2,1,0:T(2,128)(2,1)S(1)} %all-to-all-done.1) | data formatting | bytes 262144
  82.9 1.9 %shard_map.85 = bf16[64,1024]{1,0:T(8,128)(2,1)} custom-call(bf16[16,64,64]{2,1,0:T(8,128)(2,1)} %reshape.133.blocks_ref), custom_call_target="tpu_custom_call" | custom-call | tf_op jit(solution)/shard_map/pallas_call | solution.py:84
  (19 shorter events, 0.2 us)
Async XLA Ops:
  0.6 1.6 %copy-start = (bf16[4096,256]{1,0:T(8,128)(2,1)S(1)}, bf16[4096,256]{1,0:T(8,128)(2,1)}, u32[]{:S(2)}) copy-start(bf16[4096,256]{1,0:T(8,128)(2,1)} %param.9) | copy-start | bytes 6291460
  8.5 9.6 %copy-start.2 = (f32[16,256]{1,0:T(8,128)S(1)}, f32[16,256]{1,0:T(8,128)}, u32[]{:S(2)}) copy-start(f32[16,256]{1,0:T(8,128)} %param.11) | copy-start | bytes 49156
  8.5 9.6 %copy-start.1 = (f32[16,256]{1,0:T(8,128)S(1)}, f32[16,256]{1,0:T(8,128)}, u32[]{:S(2)}) copy-start(f32[16,256]{1,0:T(8,128)} %param.10) | copy-start | bytes 49156
  9.6 25.0 %all-to-all-start = ((bf16[16,64,256]{2,1,0:T(8,128)(2,1)}), bf16[16,64,256]{2,1,0:T(8,128)(2,1)S(1)}, u32[]{:S(2)}, u32[]{:S(2)}) async-start(bf16[16,64,256]{2,1,0:T(8,128)(2,1)} %bitcast.3), calls=%async_computation | async-start | bytes 1048576 | tf_op jit(solution)/shard_map/all_to_all | solution.py:55
  34.7 18.2 %collective-permute-start = (bf16[96,256]{1,0:T(8,128)(2,1)S(1)}, bf16[96,256]{1,0:T(8,128)(2,1)S(1)}, u32[]{:S(2)}, u32[]{:S(2)}) collective-permute-start(bf16[96,256]{1,0:T(8,128)(2,1)S(1)} %pad_maximum_fusion.1), channel_id=1, source_target_pairs={{0,128},{16,144},{32,160},{48,176},{64,192},{80,208},{96,224},{112... | collective-permute-start | bytes 147464 | tf_op jit(solution)/shard_map/ppermute | solution.py:60
  53.0 13.8 %collective-permute-start.1 = (bf16[128,256]{1,0:T(8,128)(2,1)S(1)}, bf16[128,256]{1,0:T(8,128)(2,1)S(1)}, u32[]{:S(2)}, u32[]{:S(2)}) collective-permute-start(bf16[128,256]{1,0:T(8,128)(2,1)S(1)} %pad_maximum_fusion), channel_id=1, source_target_pairs={{0,64},{16,80},{32,96},{48,112},{64,0},{80,16},{96,32},{112,48},{1... | collective-permute-start | bytes 196616 | tf_op jit(solution)/shard_map/ppermute | solution.py:60
  68.2 13.7 %all-to-all-start.1 = ((bf16[16,2,2048]{2,1,0:T(2,128)(2,1)}), bf16[16,2,2048]{2,1,0:T(2,128)(2,1)S(1)}, u32[]{:S(2)}, u32[]{:S(2)}) async-start(bf16[16,2,2048]{2,1,0:T(2,128)(2,1)} %reshape.132), calls=%async_computation.1 | async-start | bytes 262144 | tf_op jit(solution)/shard_map/all_to_all | solution.py:83

commit v2 on v1

--- a/solution.py
+++ b/solution.py
@@ -1,3 +1,4 @@
+import functools
 import math
 
 import jax
@@ -14,8 +15,12 @@
 adam_eps = 1e-08
 
 NEAR = [[16 * x + 4 * a + b for x in range(4) for b in range(4)] for a in range(4)]
+FAR = [[16 * x + 4 * a + b for a in range(4)] for x in range(4) for b in range(4)]
 SWAP_EIGHT = [(d, d ^ 8) for d in range(64)]
 SWAP_FOUR = [(d, d ^ 4) for d in range(64)]
+
+
+WIDTH_STEP = 1024
 
 
 def adam(first, second, gradient):
@@ -25,33 +30,110 @@
     return new_first, new_second, direction.astype(jnp.bfloat16)
 
 
+def term_kernel(factor, mask_ref, cot_hbm, act_hbm, proj_hbm, parts_ref, cot, act, turned, proj, total, cot_sem, act_sem, proj_sem):
+    tokens, width = cot.shape
+    hidden, rank = act.shape[1], proj.shape[1]
+    pieces = width // WIDTH_STEP
+
+    def cot_copy(k):
+        at = (slice(None), pl.ds(k * WIDTH_STEP, WIDTH_STEP))
+        return pltpu.make_async_copy(cot_hbm.at[at], cot.at[at], cot_sem.at[k])
+
+    def proj_copy(k):
+        at = pl.ds(k * WIDTH_STEP, WIDTH_STEP)
+        return pltpu.make_async_copy(proj_hbm.at[at], proj.at[at], proj_sem.at[k])
+
+    act_copy = pltpu.make_async_copy(act_hbm, act, act_sem)
+    ahead = 2
+
+    def start(k):
+        if k < pieces:
+            proj_copy(k).start()
+            cot_copy(k).start()
+        if k == 0:
+            act_copy.start()
+
+    for k in range(ahead):
+        start(k)
+    ones = jnp.ones((8, rank), jnp.bfloat16)
+    mask = jnp.broadcast_to(mask_ref[...].astype(jnp.float32)[None, :], (8, tokens))
+    mask8 = jnp.where(lax.broadcasted_iota(jnp.int32, mask.shape, 0) == 0, mask, 0.0)
+    live = lax.dot_general(
+        mask8.astype(jnp.bfloat16), ones, (((0,), (0,)), ((), ())), preferred_element_type=jnp.float32
+    )
+    for k in range(pieces):
+        proj_copy(k).wait()
+        cot_copy(k).wait()
+        start(k + ahead)
+        columns = slice(k * WIDTH_STEP, (k + 1) * WIDTH_STEP)
+        piece = jnp.dot(cot[:, columns], proj[columns, :], preferred_element_type=jnp.float32)
+        if k > 0:
+            piece = total[...] + piece
+        if k < pieces - 1:
+            total[...] = piece
+        if k == 0:
+            act_copy.wait()
+        if k >= 0:
+            each = hidden // (pieces - 0)
+            units = slice((k - 0) * each, (k - 0 + 1) * each)
+            turned[units, :] = act[:, units].T
+    weighted = (piece * live).astype(jnp.bfloat16)
+    for x in range(4):
+        units = slice(x * hidden // 4, (x + 1) * hidden // 4)
+        piece = jnp.dot(turned[units, :], weighted, preferred_element_type=jnp.float32)
+        done = (piece * factor).astype(jnp.bfloat16).reshape(4, 4, hidden // 64, rank)
+        for b in range(4):
+            parts_ref[4 * x + b] = done[:, b].reshape(hidden // 16, rank)
+
+
 def order_kernel(blocks_ref, update_ref):
-    _, _, length = blocks_ref.shape
-    rows = length // 4
-    source = lax.broadcasted_iota(jnp.int32, (length, 4 * length), 0)
-    target = lax.broadcasted_iota(jnp.int32, (length, 4 * length), 1)
-    start = (source // rows) * length + source % rows
-    for x in range(4):
+    _, half, length = blocks_ref.shape
+    units = length // 2
+    rows = units // 4
+    source = lax.broadcasted_iota(jnp.int32, (length, 4 * units), 0)
+    target = lax.broadcasted_iota(jnp.int32, (length, 4 * units), 1)
+    for side in range(2):
+        inside = source - side * units
+        start = (inside // rows) * units + inside % rows
+        valid = (inside >= 0) & (inside < units)
         total = None
         for b in range(4):
-            place = (target == start + b * rows).astype(jnp.bfloat16)
-            moved = jnp.dot(blocks_ref[4 * x + b], place, preferred_element_type=jnp.float32)
+            place = (valid & (target == start + b * rows)).astype(jnp.float32).astype(jnp.bfloat16)
+            stacked = jnp.concatenate([blocks_ref[4 * x + b] for x in range(4)], axis=0)
+            moved = jnp.dot(stacked, place, preferred_element_type=jnp.float32)
             total = moved if total is None else total + moved
-        update_ref[:, x * 4 * length : (x + 1) * 4 * length] = total.astype(jnp.bfloat16)
+        total = total.astype(jnp.bfloat16)
+        for x in range(4):
+            update_ref[side * half : (side + 1) * half, x * 4 * units : (x + 1) * 4 * units] = total[
+                x * half : (x + 1) * half, :
+            ]
 
 
 def per_device(cotangent, activations, live_mask, projector, first_moment, second_moment):
     width, rank = projector.shape
     own = lax.axis_index("dp")
-    projected = jnp.dot(cotangent, projector, preferred_element_type=jnp.float32)
-    weighted = (projected * live_mask.astype(jnp.float32)[:, None]).astype(jnp.bfloat16)
-    factor = 1.0 / math.sqrt(activations.shape[0] * lax.axis_size("dp"))
-    term = lax.dot_general(
-        activations, weighted, (((0,), (0,)), ((), ())), preferred_element_type=jnp.float32
-    )
-    rows = term.shape[0] // 64
-    term = (term * jnp.float32(factor)).astype(jnp.bfloat16)
-    parts = term.reshape(4, 4, 4, rows, rank).transpose(0, 2, 1, 3, 4).reshape(16, 4 * rows, rank)
+    tokens, hidden = activations.shape
+    rows, pieces = hidden // 64, width // WIDTH_STEP
+    factor = 1.0 / math.sqrt(tokens * lax.axis_size("dp"))
+    vmem, hbm = pl.BlockSpec(memory_space=pltpu.VMEM), pl.BlockSpec(memory_space=pltpu.HBM)
+    parts = pl.pallas_call(
+        functools.partial(term_kernel, factor),
+        out_shape=jax.ShapeDtypeStruct((16, 4 * rows, rank), jnp.bfloat16),
+        in_specs=[vmem, hbm, hbm, hbm],
+        out_specs=vmem,
+        scratch_shapes=[
+            pltpu.VMEM((tokens, width), jnp.bfloat16),
+            pltpu.VMEM((tokens, hidden), jnp.bfloat16),
+            pltpu.VMEM((hidden, tokens), jnp.bfloat16),
+            pltpu.VMEM((width, rank), jnp.bfloat16),
+            pltpu.VMEM((tokens, rank), jnp.float32),
+            pltpu.SemaphoreType.DMA((pieces,)),
+            pltpu.SemaphoreType.DMA,
+            pltpu.SemaphoreType.DMA((pieces,)),
+        ],
+        compiler_params=pltpu.CompilerParams(vmem_limit_bytes=60 * 2**20),
+        name="term",
+    )(live_mask, cotangent, activations, projector)
     parts = lax.all_to_all(parts, "dp", 0, 0, axis_index_groups=NEAR, tiled=True)
     partial = jnp.sum(parts.astype(jnp.float32), axis=0)
 
@@ -79,13 +161,16 @@
     bands = lax.dynamic_index_in_dim(projector.reshape(4, 4, 4, band, rank), own_far, 1, False)
     blocks = lax.dot_general(
         bands.reshape(16 * band, rank), direction, (((1,), (1,)), ((), ())), preferred_element_type=jnp.float32
-    ).astype(jnp.bfloat16).reshape(16, band, 4 * rows)
+    ).astype(jnp.bfloat16).reshape(16, 2, band // 2, 4 * rows)
+    blocks = jnp.concatenate([blocks[:, 0], blocks[:, 1]], axis=-1)
     blocks = lax.all_to_all(blocks, "dp", 0, 0, axis_index_groups=NEAR, tiled=True)
     update = pl.pallas_call(
         order_kernel,
         out_shape=jax.ShapeDtypeStruct((band, 64 * rows), jnp.bfloat16),
-        in_specs=[pl.BlockSpec(memory_space=pltpu.VMEM)],
-        out_specs=pl.BlockSpec(memory_space=pltpu.VMEM),
+        in_specs=[vmem],
+        out_specs=vmem,
+        compiler_params=pltpu.CompilerParams(vmem_limit_bytes=4 * 2**20),
+        name="order",
     )(blocks)
     return (new_first, new_second, update)
 

time: 85.2 us -> 82 us (0.962)
  Pallas kernels: 1.89 us -> 8.69 us
  matrix products: 6.55 us -> 0.27 us
  local copies, waits for them, and re-layouts: 5.12 us -> 2.53 us
  waiting for transfers between devices: 30.5 us -> 29.5 us
    pallas_call x0 -> x1, Pallas kernels: none -> 7.73 us  [per_device(): pl.pallas_call(functools.partial(term_kernel, factor), out_shape=jax.Shap...]
    dot_general x1 -> x0, matrix products: 6.28 us -> none  [per_device(): lax.dot_general(activations, weighted, (((0,), (0,)), ((), ())), preferre...]
    unnamed x8 -> x4, local copies, waits for them, and re-layouts: 2.61 us -> 0.01 us
    dynamic_slice x1, local copies, waits for them, and re-layouts: 0.04 us -> 1.09 us  [per_device(): lax.dynamic_index_in_dim(projector.reshape(4, 4, 4, band, rank), own_far,...]
    ppermute x2, waiting for transfers between devices: 6.9 us -> 5.86 us  [swap(): other = lax.ppermute(note, 'dp', pairs).astype(jnp.float32)]
    pallas_call x1, Pallas kernels: 1.89 us -> 0.96 us  [per_device(): pl.pallas_call(order_kernel, out_shape=jax.ShapeDtypeStruct((band, 64 * r...]
    transpose x1 -> x0, local copies, waits for them, and re-layouts: 0.85 us -> none  [per_device(): term.reshape(4, 4, 4, rows, rank).transpose(0, 2, 1, 3, 4)]
  transfers between devices with their start and end apart: 4 -> 4, of which waited for: 4 -> 4; matrix products, arithmetic and copies ran while one was open for 2% -> 3% of each run, Pallas kernels for 0% -> 0%
where the time goes in v2:
time: 82 us; the launch traced here: 81.6 us
  starting transfers between devices  38.7 us (47%)
  waiting for transfers between devices  29.5 us (36%)
  Pallas kernels  8.69 us (11%)
  local copies, waits for them, and re-layouts  2.53 us (3%)
  other arithmetic  0.98 us (1%)
  between operations  0.93 us (1%)
    ppermute x2, starting transfers between devices, swap(): other = lax.ppermute(note, 'dp', pairs).astype(jnp.float32)  24.9 us
    all_to_all x1, waiting for transfers between devices, per_device(): lax.all_to_all(parts, 'dp', 0, 0, axis_index_groups=NEAR, tiled=True)  16.5 us
    all_to_all x1, starting transfers between devices, per_device(): lax.all_to_all(parts, 'dp', 0, 0, axis_index_groups=NEAR, tiled=True)  8.48 us
    pallas_call x1, Pallas kernels, per_device(): pl.pallas_call(functools.partial(term_kernel, factor), out_shape=jax.Shap...  7.73 us
    all_to_all x1, waiting for transfers between devices, per_device(): lax.all_to_all(blocks, 'dp', 0, 0, axis_index_groups=NEAR, tiled=True)  7.17 us
    ppermute x2, waiting for transfers between devices, swap(): other = lax.ppermute(note, 'dp', pairs).astype(jnp.float32)  5.86 us
    all_to_all x1, starting transfers between devices, per_device(): lax.all_to_all(blocks, 'dp', 0, 0, axis_index_groups=NEAR, tiled=True)  5.28 us
  transfers between devices with their start and end apart: 4, of which 4 were waited for; matrix products, arithmetic and copies ran while one was open for 3% of the time, Pallas kernels for 0%

profile of v2, /device:TPU:24, one launch (start us, length us, event | category | flops | bytes accessed | tf_op | source)
XLA Modules:
  0.0 81.6 jit_solution(4339098358708048302)
XLA Ops:
  0.6 0.0 copy-start.1
  0.6 0.0 copy-start
  0.7 7.7 %term.1 = bf16[16,64,256]{2,1,0:T(8,128)(2,1)} custom-call(s32[768]{0:T(1024)} %mask_ref.1, bf16[768,4096]{1,0:T(8,128)(2,1)} %cot_hbm.1, bf16[768,1024]{1,0:T(8,128)(2,1)} %act_hbm.1, bf16[4096,256]{1,0:T(8,128)(2,1)} %proj_hbm.1), custom_call_target="tpu_custom_call" | custom-call | tf_op jit(solution)/shard_map/term/pallas_call | solution.py:119
  8.4 8.5 %all-to-all-start = ((bf16[16,64,256]{2,1,0:T(8,128)(2,1)}), bf16[16,64,256]{2,1,0:T(8,128)(2,1)S(1)}, u32[]{:S(2)}, u32[]{:S(2)}) async-start(bf16[16,64,256]{2,1,0:T(8,128)(2,1)} %term.1), calls=%async_computation | async-start | bytes 1048576 | tf_op jit(solution)/shard_map/all_to_all | solution.py:137
  16.9 0.0 copy-done.1
  16.9 0.0 copy-done
  16.9 16.5 %all-to-all-done = bf16[16,64,256]{2,1,0:T(8,128)(2,1)S(1)} async-done(((bf16[16,64,256]{2,1,0:T(8,128)(2,1)}), bf16[16,64,256]{2,1,0:T(8,128)(2,1)S(1)}, u32[]{:S(2)}, u32[]{:S(2)}) %all-to-all-start) | async-done | bytes 524320 | tf_op jit(solution)/shard_map/all_to_all | solution.py:137
  33.4 0.1 convert_reduce_fusion
  33.5 15.7 %collective-permute-start = (bf16[96,256]{1,0:T(8,128)(2,1)S(1)}, bf16[96,256]{1,0:T(8,128)(2,1)S(1)}, u32[]{:S(2)}, u32[]{:S(2)}) collective-permute-start(bf16[96,256]{1,0:T(8,128)(2,1)S(1)} %pad_maximum_fusion.2), channel_id=1, source_target_pairs={{0,128},{16,144},{32,160},{48,176},{64,192},{80,208},{96,224},{112... | collective-permute-start | bytes 147464 | tf_op jit(solution)/shard_map/ppermute | solution.py:142
  49.3 2.4 %collective-permute-done = bf16[96,256]{1,0:T(8,128)(2,1)S(1)} collective-permute-done((bf16[96,256]{1,0:T(8,128)(2,1)S(1)}, bf16[96,256]{1,0:T(8,128)(2,1)S(1)}, u32[]{:S(2)}, u32[]{:S(2)}) %collective-permute-start) | collective-permute-done | bytes 49184 | tf_op jit(solution)/shard_map/ppermute | solution.py:142
  51.8 9.2 %collective-permute-start.1 = (bf16[128,256]{1,0:T(8,128)(2,1)S(1)}, bf16[128,256]{1,0:T(8,128)(2,1)S(1)}, u32[]{:S(2)}, u32[]{:S(2)}) collective-permute-start(bf16[128,256]{1,0:T(8,128)(2,1)S(1)} %pad_maximum_fusion.1), channel_id=1, source_target_pairs={{0,64},{16,80},{32,96},{48,112},{64,0},{80,16},{96,32},{112,48},{1... | collective-permute-start | bytes 196616 | tf_op jit(solution)/shard_map/ppermute | solution.py:142
  61.0 1.1 %constant_dynamic-slice_fusion = bf16[4,1,4,64,256]{4,3,2,1,0:T(8,128)(2,1)S(1)} fusion(bf16[4,4,4,64,256]{4,3,2,1,0:T(8,128)(2,1)} %bitcast.34, s32[]{:T(128)S(6)} %select_n.119), kind=kLoop, calls=%fused_computation.31 | loop fusion | bytes 1048580 | tf_op jit(solution)/shard_map/jit(dynamic_index_in_dim)/dynamic_slice | solution.py:161
  62.1 3.5 %collective-permute-done.1 = bf16[128,256]{1,0:T(8,128)(2,1)S(1)} collective-permute-done((bf16[128,256]{1,0:T(8,128)(2,1)S(1)}, bf16[128,256]{1,0:T(8,128)(2,1)S(1)}, u32[]{:S(2)}, u32[]{:S(2)}) %collective-permute-start.1) | collective-permute-done | bytes 65568 | tf_op jit(solution)/shard_map/ppermute | solution.py:142
  65.7 0.3 convolution_convert_fusion
  66.0 0.2 copy.11
  66.2 0.8 pad_maximum_fusion
  66.9 5.3 %all-to-all-start.1 = ((bf16[16,32,128]{2,1,0:T(8,128)(2,1)}), bf16[16,32,128]{2,1,0:T(8,128)(2,1)S(1)}, u32[]{:S(2)}, u32[]{:S(2)}) async-start(bf16[16,32,128]{2,1,0:T(8,128)(2,1)} %pad_maximum_fusion), calls=%async_computation.1 | async-start | bytes 262144 | tf_op jit(solution)/shard_map/all_to_all | solution.py:166
  72.2 0.6 constant_dynamic-slice_fusion.2
  72.8 0.6 constant_dynamic-slice_fusion.1
  73.4 7.2 %all-to-all-done.1.blocks_ref = bf16[16,32,128]{2,1,0:T(8,128)(2,1)S(1)} async-done(((bf16[16,32,128]{2,1,0:T(8,128)(2,1)}), bf16[16,32,128]{2,1,0:T(8,128)(2,1)S(1)}, u32[]{:S(2)}, u32[]{:S(2)}) %all-to-all-start.1) | async-done | bytes 131104 | tf_op jit(solution)/shard_map/all_to_all | solution.py:166
  80.6 1.0 %order.1 = bf16[64,1024]{1,0:T(8,128)(2,1)} custom-call(bf16[16,32,128]{2,1,0:T(8,128)(2,1)S(1)} %all-to-all-done.1.blocks_ref), custom_call_target="tpu_custom_call" | custom-call | tf_op jit(solution)/shard_map/order/pallas_call | solution.py:167
  (19 shorter events, 0.2 us)
Async XLA Ops:
  0.6 16.2 %copy-start.1 = (f32[16,256]{1,0:T(8,128)S(1)}, f32[16,256]{1,0:T(8,128)}, u32[]{:S(2)}) copy-start(f32[16,256]{1,0:T(8,128)} %param.11) | copy-start | bytes 49156
  0.6 16.3 %copy-start = (f32[16,256]{1,0:T(8,128)S(1)}, f32[16,256]{1,0:T(8,128)}, u32[]{:S(2)}) copy-start(f32[16,256]{1,0:T(8,128)} %param.10) | copy-start | bytes 49156
  8.4 25.0 %all-to-all-start = ((bf16[16,64,256]{2,1,0:T(8,128)(2,1)}), bf16[16,64,256]{2,1,0:T(8,128)(2,1)S(1)}, u32[]{:S(2)}, u32[]{:S(2)}) async-start(bf16[16,64,256]{2,1,0:T(8,128)(2,1)} %term.1), calls=%async_computation | async-start | bytes 1048576 | tf_op jit(solution)/shard_map/all_to_all | solution.py:137
  33.5 18.2 %collective-permute-start = (bf16[96,256]{1,0:T(8,128)(2,1)S(1)}, bf16[96,256]{1,0:T(8,128)(2,1)S(1)}, u32[]{:S(2)}, u32[]{:S(2)}) collective-permute-start(bf16[96,256]{1,0:T(8,128)(2,1)S(1)} %pad_maximum_fusion.2), channel_id=1, source_target_pairs={{0,128},{16,144},{32,160},{48,176},{64,192},{80,208},{96,224},{112... | collective-permute-start | bytes 147464 | tf_op jit(solution)/shard_map/ppermute | solution.py:142
  51.8 13.8 %collective-permute-start.1 = (bf16[128,256]{1,0:T(8,128)(2,1)S(1)}, bf16[128,256]{1,0:T(8,128)(2,1)S(1)}, u32[]{:S(2)}, u32[]{:S(2)}) collective-permute-start(bf16[128,256]{1,0:T(8,128)(2,1)S(1)} %pad_maximum_fusion.1), channel_id=1, source_target_pairs={{0,64},{16,80},{32,96},{48,112},{64,0},{80,16},{96,32},{112,48},{1... | collective-permute-start | bytes 196616 | tf_op jit(solution)/shard_map/ppermute | solution.py:142
  66.9 13.7 %all-to-all-start.1 = ((bf16[16,32,128]{2,1,0:T(8,128)(2,1)}), bf16[16,32,128]{2,1,0:T(8,128)(2,1)S(1)}, u32[]{:S(2)}, u32[]{:S(2)}) async-start(bf16[16,32,128]{2,1,0:T(8,128)(2,1)} %pad_maximum_fusion), calls=%async_computation.1 | async-start | bytes 262144 | tf_op jit(solution)/shard_map/all_to_all | solution.py:166

commit v3 on v2

--- a/solution.py
+++ b/solution.py
@@ -86,6 +86,43 @@
             parts_ref[4 * x + b] = done[:, b].reshape(hidden // 16, rank)
 
 
+def step_kernel(sums_ref, first_ref, second_ref, other_ref, bands_ref, new_first_ref, new_second_ref, blocks_ref):
+    own_far = (lax.axis_index("dp") // 4) % 4
+    mine = own_far % 2
+    units, rank = sums_ref.shape
+    rows = units // 4
+    directions = []
+    for a in range(4):
+        here = mine == a % 2
+        at = slice((a // 2) * rows, (a // 2 + 1) * rows)
+        gradient = sums_ref[a * rows : (a + 1) * rows, :] + other_ref[a * rows : (a + 1) * rows, :].astype(jnp.float32)
+        start = units + (a // 2) * rows
+        yours = other_ref[start : start + rows, :].astype(jnp.float32)
+        first = jnp.where(here, first_ref[at, :], yours)
+        yours = other_ref[start + 2 * rows : start + 3 * rows, :].astype(jnp.float32)
+        second = jnp.where(here, second_ref[at, :], yours)
+        new_first, new_second, direction = adam(first, second, gradient)
+        directions.append(direction)
+        if a == 0:
+            own_first, own_second = new_first, new_second
+        else:
+            own_first = jnp.where(own_far == a, new_first, own_first)
+            own_second = jnp.where(own_far == a, new_second, own_second)
+    new_first_ref[...] = own_first
+    new_second_ref[...] = own_second
+    direction = jnp.concatenate(directions, axis=0)
+    none = jnp.zeros_like(direction)
+    low, high = jnp.concatenate([direction, none], axis=0), jnp.concatenate([none, direction], axis=0)
+    peers, band, _ = bands_ref.shape
+    half = band // 2
+    down = (((1,), (1,)), ((), ()))
+    top = bands_ref[:, :half, :].reshape(peers * half, rank)
+    bottom = bands_ref[:, half:, :].reshape(peers * half, rank)
+    both = lax.dot_general(top, low, down, preferred_element_type=jnp.float32)
+    both += lax.dot_general(bottom, high, down, preferred_element_type=jnp.float32)
+    blocks_ref[...] = both.astype(jnp.bfloat16).reshape(peers, half, 2 * units)
+
+
 def order_kernel(blocks_ref, update_ref):
     _, half, length = blocks_ref.shape
     units = length // 2
@@ -137,32 +174,35 @@
     parts = lax.all_to_all(parts, "dp", 0, 0, axis_index_groups=NEAR, tiled=True)
     partial = jnp.sum(parts.astype(jnp.float32), axis=0)
 
-    def swap(pairs, sums, first, second, low):
+    def swap(pairs, sums, first, second):
         note = jnp.concatenate([sums, first, second], axis=0).astype(jnp.bfloat16)
-        other = lax.ppermute(note, "dp", pairs).astype(jnp.float32)
-        ends = (sums.shape[0], sums.shape[0] + first.shape[0])
-        firsts, seconds = other[ends[0] : ends[1]], other[ends[1] :]
-
-        def pair(mine, yours):
-            mine, yours = mine.reshape(-1, rows, rank), yours.reshape(-1, rows, rank)
-            both = jnp.stack([jnp.where(low, mine, yours), jnp.where(low, yours, mine)], axis=1)
-            return both.reshape(-1, rank)
-
-        return sums + other[: ends[0]], pair(first, firsts), pair(second, seconds)
-
-    low_eight, low_four = (own // 8) % 2 == 0, (own // 4) % 2 == 0
-    gradient, firsts, seconds = swap(SWAP_EIGHT, partial, first_moment, second_moment, low_eight)
-    gradient, firsts, seconds = swap(SWAP_FOUR, gradient, firsts, seconds, low_four)
-    all_first, all_second, direction = adam(firsts, seconds, gradient)
+        return lax.ppermute(note, "dp", pairs)
+
+    other = swap(SWAP_EIGHT, partial, first_moment, second_moment).astype(jnp.float32)
+    sums = partial + other[: 4 * rows]
     own_far = (own // 4) % 4
-    new_first = lax.dynamic_slice_in_dim(all_first, own_far * rows, rows, 0)
-    new_second = lax.dynamic_slice_in_dim(all_second, own_far * rows, rows, 0)
+    low = own_far < 2
+
+    def pair(mine, yours):
+        return jnp.concatenate([jnp.where(low, mine, yours), jnp.where(low, yours, mine)], axis=0)
+
+    first = pair(first_moment, other[4 * rows : 5 * rows])
+    second = pair(second_moment, other[5 * rows :])
+    other = swap(SWAP_FOUR, sums, first, second)
     band = width // 64
     bands = lax.dynamic_index_in_dim(projector.reshape(4, 4, 4, band, rank), own_far, 1, False)
-    blocks = lax.dot_general(
-        bands.reshape(16 * band, rank), direction, (((1,), (1,)), ((), ())), preferred_element_type=jnp.float32
-    ).astype(jnp.bfloat16).reshape(16, 2, band // 2, 4 * rows)
-    blocks = jnp.concatenate([blocks[:, 0], blocks[:, 1]], axis=-1)
+    new_first, new_second, blocks = pl.pallas_call(
+        step_kernel,
+        out_shape=[
+            jax.ShapeDtypeStruct((rows, rank), jnp.float32),
+            jax.ShapeDtypeStruct((rows, rank), jnp.float32),
+            jax.ShapeDtypeStruct((16, band // 2, 8 * rows), jnp.bfloat16),
+        ],
+        in_specs=[vmem] * 5,
+        out_specs=[vmem] * 3,
+        compiler_params=pltpu.CompilerParams(vmem_limit_bytes=8 * 2**20),
+        name="step",
+    )(sums, first, second, other, bands.reshape(16, band, rank))
     blocks = lax.all_to_all(blocks, "dp", 0, 0, axis_index_groups=NEAR, tiled=True)
     update = pl.pallas_call(
         order_kernel,

time: 82 us -> 81.3 us (level)
  blocking collectives: 0 us -> 13.5 us
  waiting for transfers between devices: 29.5 us -> 22.3 us
  starting transfers between devices: 38.7 us -> 33.4 us
  local copies, waits for them, and re-layouts: 2.53 us -> 1.09 us
  Pallas kernels: 8.69 us -> 9.57 us
  other arithmetic: 0.98 us -> 0.15 us
    all_to_all x0 -> x1, blocking collectives: none -> 13.5 us  [per_device(): lax.all_to_all(blocks, 'dp', 0, 0, axis_index_groups=NEAR, tiled=True)]
    all_to_all x1 -> x0, waiting for transfers between devices: 7.17 us -> none  [per_device(): lax.all_to_all(blocks, 'dp', 0, 0, axis_index_groups=NEAR, tiled=True)]
    all_to_all x1 -> x0, starting transfers between devices: 5.28 us -> none  [per_device(): lax.all_to_all(blocks, 'dp', 0, 0, axis_index_groups=NEAR, tiled=True)]
    dynamic_slice x2 -> x0, local copies, waits for them, and re-layouts: 1.22 us -> none  [the longest x1 0.61 us: per_device(): new_first = lax.dynamic_slice_in_dim(all_first, own_far * rows, rows, 0)]
    pallas_call x0 -> x1, Pallas kernels: none -> 0.88 us  [per_device(): pl.pallas_call(step_kernel, out_shape=[jax.ShapeDtypeStruct((rows, rank),...]
  transfers between devices with their start and end apart: 4 -> 3, of which waited for: 4 -> 3; matrix products, arithmetic and copies ran while one was open for 3% -> 1% of each run, Pallas kernels for 0% -> 0%
where the time goes in v3:
time: 81.3 us; the launch traced here: 80.8 us
  starting transfers between devices  33.4 us (41%)
  waiting for transfers between devices  22.3 us (27%)
  blocking collectives  13.5 us (17%)
  Pallas kernels  9.57 us (12%)
  local copies, waits for them, and re-layouts  1.09 us (1%)
  between operations  0.83 us (1%)
    ppermute x2, starting transfers between devices, swap(): return lax.ppermute(note, 'dp', pairs)  24.9 us
    all_to_all x1, waiting for transfers between devices, per_device(): lax.all_to_all(parts, 'dp', 0, 0, axis_index_groups=NEAR, tiled=True)  16.4 us
    all_to_all x1, blocking collectives, per_device(): lax.all_to_all(blocks, 'dp', 0, 0, axis_index_groups=NEAR, tiled=True)  13.5 us
    all_to_all x1, starting transfers between devices, per_device(): lax.all_to_all(parts, 'dp', 0, 0, axis_index_groups=NEAR, tiled=True)  8.48 us
    pallas_call x1, Pallas kernels, per_device(): pl.pallas_call(functools.partial(term_kernel, factor), out_shape=jax.Shap...  7.73 us
    ppermute x2, waiting for transfers between devices, swap(): return lax.ppermute(note, 'dp', pairs)  5.91 us
  transfers between devices with their start and end apart: 3, of which 3 were waited for; matrix products, arithmetic and copies ran while one was open for 1% of the time, Pallas kernels for 0%

profile of v3, /device:TPU:24, one launch (start us, length us, event | category | flops | bytes accessed | tf_op | source)
XLA Modules:
  0.0 80.8 jit_solution(10922033949099009900)
XLA Ops:
  0.6 0.0 copy-start.1
  0.6 0.0 copy-start
  0.7 7.7 %term.1 = bf16[16,64,256]{2,1,0:T(8,128)(2,1)} custom-call(s32[768]{0:T(1024)} %mask_ref.1, bf16[768,4096]{1,0:T(8,128)(2,1)} %cot_hbm.1, bf16[768,1024]{1,0:T(8,128)(2,1)} %act_hbm.1, bf16[4096,256]{1,0:T(8,128)(2,1)} %proj_hbm.1), custom_call_target="tpu_custom_call" | custom-call | tf_op jit(solution)/shard_map/term/pallas_call | solution.py:156
  8.4 8.5 %all-to-all-start = ((bf16[16,64,256]{2,1,0:T(8,128)(2,1)}), bf16[16,64,256]{2,1,0:T(8,128)(2,1)S(1)}, u32[]{:S(2)}, u32[]{:S(2)}) async-start(bf16[16,64,256]{2,1,0:T(8,128)(2,1)} %term.1), calls=%async_computation | async-start | bytes 1048576 | tf_op jit(solution)/shard_map/all_to_all | solution.py:174
  16.9 0.0 copy-done.1
  16.9 0.0 copy-done
  17.0 16.4 %all-to-all-done = bf16[16,64,256]{2,1,0:T(8,128)(2,1)S(1)} async-done(((bf16[16,64,256]{2,1,0:T(8,128)(2,1)}), bf16[16,64,256]{2,1,0:T(8,128)(2,1)S(1)}, u32[]{:S(2)}, u32[]{:S(2)}) %all-to-all-start) | async-done | bytes 524320 | tf_op jit(solution)/shard_map/all_to_all | solution.py:174
  33.4 0.1 convert_reduce_fusion
  33.5 15.7 %collective-permute-start = (bf16[96,256]{1,0:T(8,128)(2,1)S(1)}, bf16[96,256]{1,0:T(8,128)(2,1)S(1)}, u32[]{:S(2)}, u32[]{:S(2)}) collective-permute-start(bf16[96,256]{1,0:T(8,128)(2,1)S(1)} %pad_maximum_fusion), channel_id=1, source_target_pairs={{0,128},{16,144},{32,160},{48,176},{64,192},{80,208},{96,224},{112... | collective-permute-start | bytes 147464 | tf_op jit(solution)/shard_map/ppermute | solution.py:179
  49.2 1.1 %constant_dynamic-slice_fusion = bf16[4,1,4,64,256]{4,3,2,1,0:T(8,128)(2,1)S(1)} fusion(bf16[4,4,4,64,256]{4,3,2,1,0:T(8,128)(2,1)} %bitcast.5, s32[]{:T(128)S(6)} %select_n.42), kind=kLoop, calls=%fused_computation.14 | loop fusion | bytes 1048580 | tf_op jit(solution)/shard_map/jit(dynamic_index_in_dim)/dynamic_slice | solution.py:193
  50.3 1.4 %collective-permute-done = bf16[96,256]{1,0:T(8,128)(2,1)S(1)} collective-permute-done((bf16[96,256]{1,0:T(8,128)(2,1)S(1)}, bf16[96,256]{1,0:T(8,128)(2,1)S(1)}, u32[]{:S(2)}, u32[]{:S(2)}) %collective-permute-start) | collective-permute-done | bytes 49184 | tf_op jit(solution)/shard_map/ppermute | solution.py:179
  51.8 9.2 %collective-permute-start.1 = (bf16[128,256]{1,0:T(8,128)(2,1)S(1)}, bf16[128,256]{1,0:T(8,128)(2,1)S(1)}, u32[]{:S(2)}, u32[]{:S(2)}) collective-permute-start(bf16[128,256]{1,0:T(8,128)(2,1)S(1)} %get-tuple-element.9), channel_id=1, source_target_pairs={{0,64},{16,80},{32,96},{48,112},{64,0},{80,16},{96,32},{112,48},{1... | collective-permute-start | bytes 196616 | tf_op jit(solution)/shard_map/ppermute | solution.py:179
  61.0 4.6 %collective-permute-done.1.other_ref = bf16[128,256]{1,0:T(8,128)(2,1)S(1)} collective-permute-done((bf16[128,256]{1,0:T(8,128)(2,1)S(1)}, bf16[128,256]{1,0:T(8,128)(2,1)S(1)}, u32[]{:S(2)}, u32[]{:S(2)}) %collective-permute-start.1) | collective-permute-done | bytes 65568 | tf_op jit(solution)/shard_map/ppermute | solution.py:179
  65.5 0.9 %step.1 = (f32[16,256]{1,0:T(8,128)}, f32[16,256]{1,0:T(8,128)}, bf16[16,32,128]{2,1,0:T(8,128)(2,1)S(1)}) custom-call(f32[64,256]{1,0:T(8,128)S(1)} %get-tuple-element.18.sums_ref, f32[32,256]{1,0:T(8,128)S(1)} %get-tuple-element.19.first_ref, f32[32,256]{1,0:T(8,128)S(1)} %get-tuple-element.20.second_ref, ...), custom_call_target="tpu_custom_call" | custom-call | tf_op jit(solution)/shard_map/step/pallas_call | solution.py:194
  66.4 13.5 %all_to_all.10.blocks_ref = bf16[16,32,128]{2,1,0:T(8,128)(2,1)S(1)} all-to-all(bf16[16,32,128]{2,1,0:T(8,128)(2,1)S(1)} %get-tuple-element.8), channel_id=1, replica_groups={{0,16,32,48,256,272,288,304,512,528,544,560,768,784,800,816},{64,80,96,..., dimensions={0} | all-to-all | bytes 262144 | tf_op jit(solution)/shard_map/all_to_all | solution.py:206
  79.9 1.0 %order.1 = bf16[64,1024]{1,0:T(8,128)(2,1)} custom-call(bf16[16,32,128]{2,1,0:T(8,128)(2,1)S(1)} %all_to_all.10.blocks_ref), custom_call_target="tpu_custom_call" | custom-call | tf_op jit(solution)/shard_map/order/pallas_call | solution.py:207
  (11 shorter events, 0.1 us)
Async XLA Ops:
  0.6 16.3 %copy-start.1 = (f32[16,256]{1,0:T(8,128)S(1)}, f32[16,256]{1,0:T(8,128)}, u32[]{:S(2)}) copy-start(f32[16,256]{1,0:T(8,128)} %param.11) | copy-start | bytes 49156
  0.6 16.3 %copy-start = (f32[16,256]{1,0:T(8,128)S(1)}, f32[16,256]{1,0:T(8,128)}, u32[]{:S(2)}) copy-start(f32[16,256]{1,0:T(8,128)} %param.10) | copy-start | bytes 49156
  8.4 25.0 %all-to-all-start = ((bf16[16,64,256]{2,1,0:T(8,128)(2,1)}), bf16[16,64,256]{2,1,0:T(8,128)(2,1)S(1)}, u32[]{:S(2)}, u32[]{:S(2)}) async-start(bf16[16,64,256]{2,1,0:T(8,128)(2,1)} %term.1), calls=%async_computation | async-start | bytes 1048576 | tf_op jit(solution)/shard_map/all_to_all | solution.py:174
  33.5 18.2 %collective-permute-start = (bf16[96,256]{1,0:T(8,128)(2,1)S(1)}, bf16[96,256]{1,0:T(8,128)(2,1)S(1)}, u32[]{:S(2)}, u32[]{:S(2)}) collective-permute-start(bf16[96,256]{1,0:T(8,128)(2,1)S(1)} %pad_maximum_fusion), channel_id=1, source_target_pairs={{0,128},{16,144},{32,160},{48,176},{64,192},{80,208},{96,224},{112... | collective-permute-start | bytes 147464 | tf_op jit(solution)/shard_map/ppermute | solution.py:179
  51.8 13.8 %collective-permute-start.1 = (bf16[128,256]{1,0:T(8,128)(2,1)S(1)}, bf16[128,256]{1,0:T(8,128)(2,1)S(1)}, u32[]{:S(2)}, u32[]{:S(2)}) collective-permute-start(bf16[128,256]{1,0:T(8,128)(2,1)S(1)} %get-tuple-element.9), channel_id=1, source_target_pairs={{0,64},{16,80},{32,96},{48,112},{64,0},{80,16},{96,32},{112,48},{1... | collective-permute-start | bytes 196616 | tf_op jit(solution)/shard_map/ppermute | solution.py:179

commit v4 on v3

--- a/solution.py
+++ b/solution.py
@@ -44,7 +44,7 @@
         return pltpu.make_async_copy(proj_hbm.at[at], proj.at[at], proj_sem.at[k])
 
     act_copy = pltpu.make_async_copy(act_hbm, act, act_sem)
-    ahead = 2
+    ahead = 3
 
     def start(k):
         if k < pieces:

time: 81.3 us -> 81.1 us (level)
  no operation moved by 1% of the time
where the time goes in v4:
time: 81.1 us; the launch traced here: 80.7 us
  starting transfers between devices  33.4 us (41%)
  waiting for transfers between devices  22.3 us (27%)
  blocking collectives  13.5 us (17%)
  Pallas kernels  9.42 us (12%)
  local copies, waits for them, and re-layouts  1.09 us (1%)
  between operations  0.83 us (1%)
    ppermute x2, starting transfers between devices, swap(): return lax.ppermute(note, 'dp', pairs)  24.9 us
    all_to_all x1, waiting for transfers between devices, per_device(): lax.all_to_all(parts, 'dp', 0, 0, axis_index_groups=NEAR, tiled=True)  16.4 us
    all_to_all x1, blocking collectives, per_device(): lax.all_to_all(blocks, 'dp', 0, 0, axis_index_groups=NEAR, tiled=True)  13.5 us
    all_to_all x1, starting transfers between devices, per_device(): lax.all_to_all(parts, 'dp', 0, 0, axis_index_groups=NEAR, tiled=True)  8.47 us
    pallas_call x1, Pallas kernels, per_device(): pl.pallas_call(functools.partial(term_kernel, factor), out_shape=jax.Shap...  7.58 us
    ppermute x2, waiting for transfers between devices, swap(): return lax.ppermute(note, 'dp', pairs)  5.91 us
  transfers between devices with their start and end apart: 3, of which 3 were waited for; matrix products, arithmetic and copies ran while one was open for 1% of the time, Pallas kernels for 0%

profile of v4, /device:TPU:24, one launch (start us, length us, event | category | flops | bytes accessed | tf_op | source)
XLA Modules:
  0.0 80.7 jit_solution(3068194193810808686)
XLA Ops:
  0.6 0.0 copy-start.1
  0.6 0.0 copy-start
  0.7 7.6 %term.1 = bf16[16,64,256]{2,1,0:T(8,128)(2,1)} custom-call(s32[768]{0:T(1024)} %mask_ref.1, bf16[768,4096]{1,0:T(8,128)(2,1)} %cot_hbm.1, bf16[768,1024]{1,0:T(8,128)(2,1)} %act_hbm.1, bf16[4096,256]{1,0:T(8,128)(2,1)} %proj_hbm.1), custom_call_target="tpu_custom_call" | custom-call | tf_op jit(solution)/shard_map/term/pallas_call | solution.py:156
  8.2 8.5 %all-to-all-start = ((bf16[16,64,256]{2,1,0:T(8,128)(2,1)}), bf16[16,64,256]{2,1,0:T(8,128)(2,1)S(1)}, u32[]{:S(2)}, u32[]{:S(2)}) async-start(bf16[16,64,256]{2,1,0:T(8,128)(2,1)} %term.1), calls=%async_computation | async-start | bytes 1048576 | tf_op jit(solution)/shard_map/all_to_all | solution.py:174
  16.8 0.0 copy-done.1
  16.8 0.0 copy-done
  16.8 16.4 %all-to-all-done = bf16[16,64,256]{2,1,0:T(8,128)(2,1)S(1)} async-done(((bf16[16,64,256]{2,1,0:T(8,128)(2,1)}), bf16[16,64,256]{2,1,0:T(8,128)(2,1)S(1)}, u32[]{:S(2)}, u32[]{:S(2)}) %all-to-all-start) | async-done | bytes 524320 | tf_op jit(solution)/shard_map/all_to_all | solution.py:174
  33.2 0.1 convert_reduce_fusion
  33.3 15.7 %collective-permute-start = (bf16[96,256]{1,0:T(8,128)(2,1)S(1)}, bf16[96,256]{1,0:T(8,128)(2,1)S(1)}, u32[]{:S(2)}, u32[]{:S(2)}) collective-permute-start(bf16[96,256]{1,0:T(8,128)(2,1)S(1)} %pad_maximum_fusion), channel_id=1, source_target_pairs={{0,128},{16,144},{32,160},{48,176},{64,192},{80,208},{96,224},{112... | collective-permute-start | bytes 147464 | tf_op jit(solution)/shard_map/ppermute | solution.py:179
  49.1 1.1 %constant_dynamic-slice_fusion = bf16[4,1,4,64,256]{4,3,2,1,0:T(8,128)(2,1)S(1)} fusion(bf16[4,4,4,64,256]{4,3,2,1,0:T(8,128)(2,1)} %bitcast.5, s32[]{:T(128)S(6)} %select_n.42), kind=kLoop, calls=%fused_computation.14 | loop fusion | bytes 1048580 | tf_op jit(solution)/shard_map/jit(dynamic_index_in_dim)/dynamic_slice | solution.py:193
  50.2 1.4 %collective-permute-done = bf16[96,256]{1,0:T(8,128)(2,1)S(1)} collective-permute-done((bf16[96,256]{1,0:T(8,128)(2,1)S(1)}, bf16[96,256]{1,0:T(8,128)(2,1)S(1)}, u32[]{:S(2)}, u32[]{:S(2)}) %collective-permute-start) | collective-permute-done | bytes 49184 | tf_op jit(solution)/shard_map/ppermute | solution.py:179
  51.6 9.2 %collective-permute-start.1 = (bf16[128,256]{1,0:T(8,128)(2,1)S(1)}, bf16[128,256]{1,0:T(8,128)(2,1)S(1)}, u32[]{:S(2)}, u32[]{:S(2)}) collective-permute-start(bf16[128,256]{1,0:T(8,128)(2,1)S(1)} %get-tuple-element.9), channel_id=1, source_target_pairs={{0,64},{16,80},{32,96},{48,112},{64,0},{80,16},{96,32},{112,48},{1... | collective-permute-start | bytes 196616 | tf_op jit(solution)/shard_map/ppermute | solution.py:179
  60.8 4.6 %collective-permute-done.1.other_ref = bf16[128,256]{1,0:T(8,128)(2,1)S(1)} collective-permute-done((bf16[128,256]{1,0:T(8,128)(2,1)S(1)}, bf16[128,256]{1,0:T(8,128)(2,1)S(1)}, u32[]{:S(2)}, u32[]{:S(2)}) %collective-permute-start.1) | collective-permute-done | bytes 65568 | tf_op jit(solution)/shard_map/ppermute | solution.py:179
  65.4 0.9 %step.1 = (f32[16,256]{1,0:T(8,128)}, f32[16,256]{1,0:T(8,128)}, bf16[16,32,128]{2,1,0:T(8,128)(2,1)S(1)}) custom-call(f32[64,256]{1,0:T(8,128)S(1)} %get-tuple-element.18.sums_ref, f32[32,256]{1,0:T(8,128)S(1)} %get-tuple-element.19.first_ref, f32[32,256]{1,0:T(8,128)S(1)} %get-tuple-element.20.second_ref, ...), custom_call_target="tpu_custom_call" | custom-call | tf_op jit(solution)/shard_map/step/pallas_call | solution.py:194
  66.3 13.5 %all_to_all.10.blocks_ref = bf16[16,32,128]{2,1,0:T(8,128)(2,1)S(1)} all-to-all(bf16[16,32,128]{2,1,0:T(8,128)(2,1)S(1)} %get-tuple-element.8), channel_id=1, replica_groups={{0,16,32,48,256,272,288,304,512,528,544,560,768,784,800,816},{64,80,96,..., dimensions={0} | all-to-all | bytes 262144 | tf_op jit(solution)/shard_map/all_to_all | solution.py:206
  79.7 1.0 %order.1 = bf16[64,1024]{1,0:T(8,128)(2,1)} custom-call(bf16[16,32,128]{2,1,0:T(8,128)(2,1)S(1)} %all_to_all.10.blocks_ref), custom_call_target="tpu_custom_call" | custom-call | tf_op jit(solution)/shard_map/order/pallas_call | solution.py:207
  (11 shorter events, 0.1 us)
Async XLA Ops:
  0.6 16.1 %copy-start.1 = (f32[16,256]{1,0:T(8,128)S(1)}, f32[16,256]{1,0:T(8,128)}, u32[]{:S(2)}) copy-start(f32[16,256]{1,0:T(8,128)} %param.11) | copy-start | bytes 49156
  0.6 16.1 %copy-start = (f32[16,256]{1,0:T(8,128)S(1)}, f32[16,256]{1,0:T(8,128)}, u32[]{:S(2)}) copy-start(f32[16,256]{1,0:T(8,128)} %param.10) | copy-start | bytes 49156
  8.2 25.0 %all-to-all-start = ((bf16[16,64,256]{2,1,0:T(8,128)(2,1)}), bf16[16,64,256]{2,1,0:T(8,128)(2,1)S(1)}, u32[]{:S(2)}, u32[]{:S(2)}) async-start(bf16[16,64,256]{2,1,0:T(8,128)(2,1)} %term.1), calls=%async_computation | async-start | bytes 1048576 | tf_op jit(solution)/shard_map/all_to_all | solution.py:174
  33.3 18.2 %collective-permute-start = (bf16[96,256]{1,0:T(8,128)(2,1)S(1)}, bf16[96,256]{1,0:T(8,128)(2,1)S(1)}, u32[]{:S(2)}, u32[]{:S(2)}) collective-permute-start(bf16[96,256]{1,0:T(8,128)(2,1)S(1)} %pad_maximum_fusion), channel_id=1, source_target_pairs={{0,128},{16,144},{32,160},{48,176},{64,192},{80,208},{96,224},{112... | collective-permute-start | bytes 147464 | tf_op jit(solution)/shard_map/ppermute | solution.py:179
  51.6 13.8 %collective-permute-start.1 = (bf16[128,256]{1,0:T(8,128)(2,1)S(1)}, bf16[128,256]{1,0:T(8,128)(2,1)S(1)}, u32[]{:S(2)}, u32[]{:S(2)}) collective-permute-start(bf16[128,256]{1,0:T(8,128)(2,1)S(1)} %get-tuple-element.9), channel_id=1, source_target_pairs={{0,64},{16,80},{32,96},{48,112},{64,0},{80,16},{96,32},{112,48},{1... | collective-permute-start | bytes 196616 | tf_op jit(solution)/shard_map/ppermute | solution.py:179

commit v5 on v4

--- a/solution.py
+++ b/solution.py
@@ -50,7 +50,7 @@
         if k < pieces:
             proj_copy(k).start()
             cot_copy(k).start()
-        if k == 0:
+        if k == 2:
             act_copy.start()
 
     for k in range(ahead):
@@ -71,11 +71,11 @@
             piece = total[...] + piece
         if k < pieces - 1:
             total[...] = piece
-        if k == 0:
+        if k == 2:
             act_copy.wait()
-        if k >= 0:
-            each = hidden // (pieces - 0)
-            units = slice((k - 0) * each, (k - 0 + 1) * each)
+        if k >= 2:
+            each = hidden // (pieces - 2)
+            units = slice((k - 2) * each, (k - 2 + 1) * each)
             turned[units, :] = act[:, units].T
     weighted = (piece * live).astype(jnp.bfloat16)
     for x in range(4):

time: 81.1 us -> 81 us (level)
  no operation moved by 1% of the time
where the time goes in v5:
time: 81 us; the launch traced here: 80.6 us
  starting transfers between devices  33.4 us (41%)
  waiting for transfers between devices  22.3 us (28%)
  blocking collectives  13.5 us (17%)
  Pallas kernels  9.28 us (11%)
  local copies, waits for them, and re-layouts  1.09 us (1%)
  between operations  0.83 us (1%)
    ppermute x2, starting transfers between devices, swap(): return lax.ppermute(note, 'dp', pairs)  24.9 us
    all_to_all x1, waiting for transfers between devices, per_device(): lax.all_to_all(parts, 'dp', 0, 0, axis_index_groups=NEAR, tiled=True)  16.4 us
    all_to_all x1, blocking collectives, per_device(): lax.all_to_all(blocks, 'dp', 0, 0, axis_index_groups=NEAR, tiled=True)  13.5 us
    all_to_all x1, starting transfers between devices, per_device(): lax.all_to_all(parts, 'dp', 0, 0, axis_index_groups=NEAR, tiled=True)  8.48 us
    pallas_call x1, Pallas kernels, per_device(): pl.pallas_call(functools.partial(term_kernel, factor), out_shape=jax.Shap...  7.44 us
    ppermute x2, waiting for transfers between devices, swap(): return lax.ppermute(note, 'dp', pairs)  5.91 us
  transfers between devices with their start and end apart: 3, of which 3 were waited for; matrix products, arithmetic and copies ran while one was open for 1% of the time, Pallas kernels for 0%

profile of v5, /device:TPU:24, one launch (start us, length us, event | category | flops | bytes accessed | tf_op | source)
XLA Modules:
  0.0 80.6 jit_solution(11185074988698389499)
XLA Ops:
  0.6 0.0 copy-start.1
  0.6 0.0 copy-start
  0.7 7.4 %term.1 = bf16[16,64,256]{2,1,0:T(8,128)(2,1)} custom-call(s32[768]{0:T(1024)} %mask_ref.1, bf16[768,4096]{1,0:T(8,128)(2,1)} %cot_hbm.1, bf16[768,1024]{1,0:T(8,128)(2,1)} %act_hbm.1, bf16[4096,256]{1,0:T(8,128)(2,1)} %proj_hbm.1), custom_call_target="tpu_custom_call" | custom-call | tf_op jit(solution)/shard_map/term/pallas_call | solution.py:156
  8.1 8.5 %all-to-all-start = ((bf16[16,64,256]{2,1,0:T(8,128)(2,1)}), bf16[16,64,256]{2,1,0:T(8,128)(2,1)S(1)}, u32[]{:S(2)}, u32[]{:S(2)}) async-start(bf16[16,64,256]{2,1,0:T(8,128)(2,1)} %term.1), calls=%async_computation | async-start | bytes 1048576 | tf_op jit(solution)/shard_map/all_to_all | solution.py:174
  16.6 0.0 copy-done.1
  16.6 0.0 copy-done
  16.7 16.4 %all-to-all-done = bf16[16,64,256]{2,1,0:T(8,128)(2,1)S(1)} async-done(((bf16[16,64,256]{2,1,0:T(8,128)(2,1)}), bf16[16,64,256]{2,1,0:T(8,128)(2,1)S(1)}, u32[]{:S(2)}, u32[]{:S(2)}) %all-to-all-start) | async-done | bytes 524320 | tf_op jit(solution)/shard_map/all_to_all | solution.py:174
  33.1 0.1 convert_reduce_fusion
  33.2 15.7 %collective-permute-start = (bf16[96,256]{1,0:T(8,128)(2,1)S(1)}, bf16[96,256]{1,0:T(8,128)(2,1)S(1)}, u32[]{:S(2)}, u32[]{:S(2)}) collective-permute-start(bf16[96,256]{1,0:T(8,128)(2,1)S(1)} %pad_maximum_fusion), channel_id=1, source_target_pairs={{0,128},{16,144},{32,160},{48,176},{64,192},{80,208},{96,224},{112... | collective-permute-start | bytes 147464 | tf_op jit(solution)/shard_map/ppermute | solution.py:179
  48.9 1.1 %constant_dynamic-slice_fusion = bf16[4,1,4,64,256]{4,3,2,1,0:T(8,128)(2,1)S(1)} fusion(bf16[4,4,4,64,256]{4,3,2,1,0:T(8,128)(2,1)} %bitcast.5, s32[]{:T(128)S(6)} %select_n.42), kind=kLoop, calls=%fused_computation.14 | loop fusion | bytes 1048580 | tf_op jit(solution)/shard_map/jit(dynamic_index_in_dim)/dynamic_slice | solution.py:193
  50.0 1.4 %collective-permute-done = bf16[96,256]{1,0:T(8,128)(2,1)S(1)} collective-permute-done((bf16[96,256]{1,0:T(8,128)(2,1)S(1)}, bf16[96,256]{1,0:T(8,128)(2,1)S(1)}, u32[]{:S(2)}, u32[]{:S(2)}) %collective-permute-start) | collective-permute-done | bytes 49184 | tf_op jit(solution)/shard_map/ppermute | solution.py:179
  51.5 9.2 %collective-permute-start.1 = (bf16[128,256]{1,0:T(8,128)(2,1)S(1)}, bf16[128,256]{1,0:T(8,128)(2,1)S(1)}, u32[]{:S(2)}, u32[]{:S(2)}) collective-permute-start(bf16[128,256]{1,0:T(8,128)(2,1)S(1)} %get-tuple-element.9), channel_id=1, source_target_pairs={{0,64},{16,80},{32,96},{48,112},{64,0},{80,16},{96,32},{112,48},{1... | collective-permute-start | bytes 196616 | tf_op jit(solution)/shard_map/ppermute | solution.py:179
  60.7 4.6 %collective-permute-done.1.other_ref = bf16[128,256]{1,0:T(8,128)(2,1)S(1)} collective-permute-done((bf16[128,256]{1,0:T(8,128)(2,1)S(1)}, bf16[128,256]{1,0:T(8,128)(2,1)S(1)}, u32[]{:S(2)}, u32[]{:S(2)}) %collective-permute-start.1) | collective-permute-done | bytes 65568 | tf_op jit(solution)/shard_map/ppermute | solution.py:179
  65.2 0.9 %step.1 = (f32[16,256]{1,0:T(8,128)}, f32[16,256]{1,0:T(8,128)}, bf16[16,32,128]{2,1,0:T(8,128)(2,1)S(1)}) custom-call(f32[64,256]{1,0:T(8,128)S(1)} %get-tuple-element.18.sums_ref, f32[32,256]{1,0:T(8,128)S(1)} %get-tuple-element.19.first_ref, f32[32,256]{1,0:T(8,128)S(1)} %get-tuple-element.20.second_ref, ...), custom_call_target="tpu_custom_call" | custom-call | tf_op jit(solution)/shard_map/step/pallas_call | solution.py:194
  66.1 13.5 %all_to_all.10.blocks_ref = bf16[16,32,128]{2,1,0:T(8,128)(2,1)S(1)} all-to-all(bf16[16,32,128]{2,1,0:T(8,128)(2,1)S(1)} %get-tuple-element.8), channel_id=1, replica_groups={{0,16,32,48,256,272,288,304,512,528,544,560,768,784,800,816},{64,80,96,..., dimensions={0} | all-to-all | bytes 262144 | tf_op jit(solution)/shard_map/all_to_all | solution.py:206
  79.6 1.0 %order.1 = bf16[64,1024]{1,0:T(8,128)(2,1)} custom-call(bf16[16,32,128]{2,1,0:T(8,128)(2,1)S(1)} %all_to_all.10.blocks_ref), custom_call_target="tpu_custom_call" | custom-call | tf_op jit(solution)/shard_map/order/pallas_call | solution.py:207
  (11 shorter events, 0.1 us)
Async XLA Ops:
  0.6 16.0 %copy-start.1 = (f32[16,256]{1,0:T(8,128)S(1)}, f32[16,256]{1,0:T(8,128)}, u32[]{:S(2)}) copy-start(f32[16,256]{1,0:T(8,128)} %param.11) | copy-start | bytes 49156
  0.6 16.0 %copy-start = (f32[16,256]{1,0:T(8,128)S(1)}, f32[16,256]{1,0:T(8,128)}, u32[]{:S(2)}) copy-start(f32[16,256]{1,0:T(8,128)} %param.10) | copy-start | bytes 49156
  8.1 25.0 %all-to-all-start = ((bf16[16,64,256]{2,1,0:T(8,128)(2,1)}), bf16[16,64,256]{2,1,0:T(8,128)(2,1)S(1)}, u32[]{:S(2)}, u32[]{:S(2)}) async-start(bf16[16,64,256]{2,1,0:T(8,128)(2,1)} %term.1), calls=%async_computation | async-start | bytes 1048576 | tf_op jit(solution)/shard_map/all_to_all | solution.py:174
  33.2 18.2 %collective-permute-start = (bf16[96,256]{1,0:T(8,128)(2,1)S(1)}, bf16[96,256]{1,0:T(8,128)(2,1)S(1)}, u32[]{:S(2)}, u32[]{:S(2)}) collective-permute-start(bf16[96,256]{1,0:T(8,128)(2,1)S(1)} %pad_maximum_fusion), channel_id=1, source_target_pairs={{0,128},{16,144},{32,160},{48,176},{64,192},{80,208},{96,224},{112... | collective-permute-start | bytes 147464 | tf_op jit(solution)/shard_map/ppermute | solution.py:179
  51.5 13.8 %collective-permute-start.1 = (bf16[128,256]{1,0:T(8,128)(2,1)S(1)}, bf16[128,256]{1,0:T(8,128)(2,1)S(1)}, u32[]{:S(2)}, u32[]{:S(2)}) collective-permute-start(bf16[128,256]{1,0:T(8,128)(2,1)S(1)} %get-tuple-element.9), channel_id=1, source_target_pairs={{0,64},{16,80},{32,96},{48,112},{64,0},{80,16},{96,32},{112,48},{1... | collective-permute-start | bytes 196616 | tf_op jit(solution)/shard_map/ppermute | solution.py:179
